TPU v7x, 32 devices: a whole 2x2x4 slice. The times are simulated.
32 devices in a mesh: parts: 2 (over x), param: 16 (over z, y, core).
Axes of the slice: x: 2, y: 2, z: 4, core: 2. Of those that a mesh axis runs over, the one named last changes fastest.
Arguments:
- inputs: bfloat16 [8192, 4096], P(('parts', 'param')), parts along dimension 0, may hold values from -7 to 7
- out_grads: bfloat16 [8192, 14336], P(('parts', 'param')), parts along dimension 0, may hold values from -7 to 7
- lengths: int32 [32], P(('parts', 'param')), parts along dimension 0, may hold values from 128 to 256, as said below
- example_ids: int32 [32], P(('parts', 'param')), parts along dimension 0, may hold values from 0 to 15, each once
- proj_seeds: int32 [4], P('parts'), parts along dimension 0, may hold values from 1 to 29999
Outputs:
- fisher: float32 [16384, 8192], P(('parts', 'param')), parts along dimension 0
- precond: float32 [32, 8192], P(('parts', 'param')), parts along dimension 0
- kernel: float32 [32, 16], P(('parts', 'param')), parts along dimension 0
There are 2 independent parts, one for each index of `parts`. A program takes and returns all parts, laid end to end along the dimension named above; each array names one. Nothing has to cross between parts.
Inputs may be any that keep to these rules, and one draw needn't show every extreme that they name: `lengths`: each length is a multiple of 128; some example has the full 256 tokens and some has only 128. `example_ids`: a permutation of the group's example indices.
All inputs are finite; a program needn't handle non-finite values.
Results may differ from a plain program's by a relative error of at most 0.007.
The roundings to bfloat16 on the way count: a program that leaves them out, or rounds other values in their place, can miss the bound.
Values may be sent and summed in bfloat16 or wider, within the bound.
A program may use at most 64 MiB of HBM per device.

v0:
```python
import math

import jax
import jax.numpy as jnp
from jax import lax
from jax.sharding import PartitionSpec as P

K_IN = 64
K_OUT = 128


damp_ratio = 0.5


def projection_table(out_dim, fan_in, seed_value):
    row_index = lax.broadcasted_iota(jnp.int32, (fan_in, out_dim), 1)
    col_index = lax.broadcasted_iota(jnp.int32, (fan_in, out_dim), 0)
    hashed = (row_index * 7919 + col_index * 3571 + seed_value * 9973) % 65521
    hashed = hashed * (hashed % 509 + 17) % 65521
    hashed = (hashed * 97 + row_index * 31 + col_index) % 65521
    uniform = hashed.astype(jnp.float32) * (2.0 / 65520.0) - 1.0
    return (uniform * math.sqrt(3.0 / fan_in)).astype(jnp.bfloat16)


def local(inputs, out_grads, lengths, example_ids, proj_seeds):
    highest = lax.Precision.HIGHEST
    ex_dev = lengths.shape[0]
    slot_len = inputs.shape[0] // ex_dev
    table_in = projection_table(K_IN, inputs.shape[1], proj_seeds[0])
    table_out = projection_table(K_OUT, out_grads.shape[1], proj_seeds[1])
    proj_in = jnp.dot(inputs, table_in, preferred_element_type=jnp.float32).astype(jnp.bfloat16)
    proj_out = jnp.dot(out_grads, table_out, preferred_element_type=jnp.float32).astype(
        jnp.bfloat16
    )
    live_rows = (lax.broadcasted_iota(jnp.int32, (ex_dev, slot_len), 1) < lengths[:, None]).reshape(
        ex_dev * slot_len, 1
    )
    proj_in = jnp.where(live_rows, proj_in, jnp.zeros_like(proj_in))
    outer = jnp.einsum(
        "esi,eso->eio",
        proj_in.reshape(ex_dev, slot_len, K_IN),
        proj_out.reshape(ex_dev, slot_len, K_OUT),
        preferred_element_type=jnp.float32,
    )
    gradients = (
        (outer * (1.0 / math.sqrt(slot_len))).reshape(ex_dev, K_IN * K_OUT).astype(jnp.bfloat16)
    )
    gathered, all_ids = (
        lax.all_gather(gradients, "param", axis=0, tiled=True),
        lax.all_gather(example_ids, "param", axis=0, tiled=True),
    )
    example_count = gathered.shape[0]
    proj_width = gathered.shape[1]
    block_rows = proj_width // lax.axis_size("param")
    column_block = lax.dynamic_slice_in_dim(
        gathered, lax.axis_index("param") * block_rows, block_rows, 1
    )
    fisher = (
        lax.dot_general(
            column_block, gathered, (((0,), (0,)), ((), ())), preferred_element_type=jnp.float32
        )
        / example_count
    )
    damping = (
        damp_ratio
        * jnp.sum(jnp.square(gathered.astype(jnp.float32)))
        / (example_count * proj_width)
    )
    gram_matrix = lax.dot_general(
        gathered, gathered, (((1,), (1,)), ((), ())), preferred_element_type=jnp.float32
    )
    system = gram_matrix + damping * example_count * jnp.eye(example_count, dtype=jnp.float32)
    factor = jnp.linalg.cholesky(system)
    solved = jax.scipy.linalg.cho_solve((factor, True), gram_matrix)
    first_slot = lax.axis_index("param") * ex_dev
    own_cols = lax.dynamic_slice_in_dim(solved, first_slot, ex_dev, 1)
    correction = jnp.einsum(
        "jr,jp->rp", own_cols, gathered, precision=highest, preferred_element_type=jnp.float32
    )
    precond = (gradients.astype(jnp.float32) - correction) / damping
    slot_numbers = lax.broadcasted_iota(jnp.int32, (example_count,), 0)
    inverse = jnp.zeros((example_count,), jnp.int32).at[all_ids].set(slot_numbers)
    own_slots = inverse[first_slot + lax.broadcasted_iota(jnp.int32, (ex_dev,), 0)]
    own_grads = jnp.take(gathered, own_slots, axis=0)
    tile_block = lax.dot_general(
        own_grads,
        lax.all_gather(precond.astype(jnp.bfloat16), "param", axis=0, tiled=True),
        (((1,), (1,)), ((), ())),
        preferred_element_type=jnp.float32,
    )
    kernel = (
        jnp.zeros((ex_dev, example_count), jnp.float32).at[:, all_ids].set(tile_block) / proj_width
    )
    return (fisher, precond, kernel)


def solution(mesh):
    placed = (
        P(("parts", "param"), None),
        P(("parts", "param"), None),
        P(("parts", "param")),
        P(("parts", "param")),
        P("parts"),
    )
    return jax.shard_map(
        local,
        mesh=mesh,
        in_specs=placed,
        out_specs=(
            P(("parts", "param"), None),
            P(("parts", "param"), None),
            P(("parts", "param"), None),
        ),
        check_vma=False,
    )
```

profile of v0, /device:TPU:0, one launch (start us, length us, event | category | flops | bytes accessed | tf_op | source)
XLA Modules:
  0.0 117.9 jit_solution(8692307448393772548)
XLA Ops:
  0.6 0.0 copy-start
  2.1 1.2 %dynamic-slice.7 = u32[1]{0:T(128)} dynamic-slice(u32[32]{0:T(128)} %constant.217, u32[]{:T(128)S(6)} %add.156), dynamic_slice_sizes={1} | dynamic-slice | bytes 12
  3.4 0.8 dynamic-update-slice.5
  4.1 13.7 %all-reduce = s32[16]{0:T(128)S(1)} all-reduce(s32[16]{0:T(128)S(1)} %dynamic-update-slice.5), channel_id=1, replica_groups=mesh['parts'=2,'param'=16] {'param'}, use_global_device_ids=true, to_apply=%add | all-reduce | flops 16 | bytes 128
  17.8 0.6 scatter_custom_fusion
  18.5 0.6 dynamic-slice.5
  21.0 1.3 %fusion.127 = (s32[1]{0:T(128)}, s32[1]{0:T(128)}) fusion(s32[2]{0:T(128)} %param.9), kind=kLoop, calls=%fused_computation.144 | loop fusion | bytes 16 | tf_op jit(solution)/shard_map/slice | solution.py:30
  23.7 0.0 copy-done
  23.7 0.0 copy-start.1
  23.7 5.3 %fusion.58 = bf16[64,256]{1,0:T(8,128)(2,1)S(1)} fusion(bf16[256,4096]{1,0:T(8,128)(2,1)S(1)} %copy-done, s32[64]{0:T(128)S(1)} %get-tuple-element.31, s32[]{:T(128)} %bitcast.1, s32[4096]{0:T(1024)S(1)} %iota_multiply_fusion.1, s32[64]{0:T(128)S(1)} %get-tuple-element.32, pred[256]{0:T(512)(128)(4,1)S(1)} %iota_compare_fusion.3), kind=kOutput, calls=%fused_computation.67 | convolution fusion | flops 143687680 | bytes 2147076 | tf_op jit(solution)/shard_map/dot_general | solution.py:31
  29.0 0.0 copy-done.1
  29.1 32.5 %fusion.52.clone.8 = bf16[128,256]{1,0:T(8,128)(2,1)S(1)} fusion(bf16[256,14336]{1,0:T(8,128)(2,1)S(1)} %copy-done.1, s32[128]{0:T(128)S(1)} %get-tuple-element.33, s32[]{:T(128)} %bitcast.2, s32[14336]{0:T(1024)S(1)} %iota_multiply_fusion, s32[128]{0:T(128)S(1)} %get-tuple-element.34), kind=kOutput, calls=%fused_computation.64.clone.clone.clone.clone.clone.clone.clone.1 | convolution fusion | flops 1005617152 | bytes 7463940 | tf_op jit(solution)/shard_map/dot_general | solution.py:32
  61.5 0.1 fusion.62
  61.7 19.4 %all-gather.1 = bf16[16,1,8192]{2,1,0:T(2,128)(2,1)S(1)} all-gather(bf16[1,1,8192]{2,1,0:T(2,128)(2,1)S(1)} %reshape.155), channel_id=1, replica_groups=mesh['parts'=2,'param'=16] {'param'}, dimensions={0}, use_global_device_ids=true | all-gather | bytes 278528 | tf_op jit(solution)/shard_map/all_gather | solution.py:49
  81.1 0.9 multiply_reduce_fusion
  83.3 0.2 fusion.78
  83.5 0.1 copy.12
  83.6 1.5 %cholesky.16 = f32[16,16]{1,0:T(8,128)S(1)} custom-call(f32[16,16]{1,0:T(8,128)S(1)} %fusion.94), custom_call_target="Cholesky" | custom-call | tf_op jit(solution)/shard_map/jit(cholesky)/cholesky | solution.py:73
  85.1 0.6 compare_reduce_fusion
  85.8 0.6 fusion.88
  86.4 1.2 %custom-call.10 = f32[1,16,16]{1,2,0:T(8,128)S(1)} custom-call(f32[1,16,16]{2,1,0:T(8,128)S(1)} %fusion.88), custom_call_target="InvertDiagBlocksLowerTriangular" | custom-call | tf_op jit(solution)/shard_map/jit(_cho_solve)/triangular_solve | solution.py:74
  87.7 0.2 fusion.91
  87.9 0.2 fusion.89
  88.1 0.3 fusion.81
  88.4 0.6 fusion.125
  89.0 19.0 %all-gather = bf16[131072]{0:T(1024)(128)(2,1)S(1)} all-gather(bf16[8192]{0:T(1024)(128)(2,1)S(1)} %get-tuple-element.25), channel_id=2, replica_groups=mesh['parts'=2,'param'=16] {'param'}, dimensions={0}, use_global_device_ids=true | all-gather | bytes 278528 | tf_op jit(solution)/shard_map/all_gather | solution.py:87
  107.9 0.1 reshape.146
  108.1 0.2 convolution_bitcast_fusion
  108.3 0.6 scatter_custom_fusion.1
  108.9 0.5 multiply_bitcast_fusion
  109.4 8.5 %convolution_multiply_fusion = f32[512,8192]{1,0:T(8,128)} fusion(bf16[16,1,8192]{2,0,1:T(8,128)(2,1)S(1)} %get-tuple-element.28, bf16[16,1,512]{2,1,0:T(2,128)(2,1)S(1)} %constant_dynamic-slice_fusion.1), kind=kOutput, calls=%fused_computation.2 | convolution fusion | flops 138412032 | bytes 17055744 | tf_op jit(solution)/shard_map/dot_general | solution.py:59
  (12 shorter events, 0.1 us)
Async XLA Ops:
  0.6 23.0 %copy-start = (bf16[256,4096]{1,0:T(8,128)(2,1)S(1)}, bf16[256,4096]{1,0:T(8,128)(2,1)}, u32[]{:S(2)}) copy-start(bf16[256,4096]{1,0:T(8,128)(2,1)} %param.5) | copy-start | bytes 6291460
  23.7 5.4 %copy-start.1 = (bf16[256,14336]{1,0:T(8,128)(2,1)S(1)}, bf16[256,14336]{1,0:T(8,128)(2,1)}, u32[]{:S(2)}) copy-start(bf16[256,14336]{1,0:T(8,128)(2,1)} %param.6) | copy-start | bytes 22020100
where the time goes:
time: 118 us
  blocking collectives  52.1 us (44%)
  matrix products  47.6 us (40%)
  between operations  6.76 us (6%)
  other arithmetic  6.11 us (5%)
  local copies, waits for them, and re-layouts  5.43 us (5%)
    dot_general x1, matrix products, local(): jnp.dot(out_grads, table_out, preferred_element_type=jnp.float32)  32.5 us
    all_gather x1, blocking collectives, local(): lax.all_gather(gradients, 'param', axis=0, tiled=True)  19.4 us
    all_gather x1, blocking collectives, local(): lax.all_gather(precond.astype(jnp.bfloat16), 'param', axis=0, tiled=True)  19 us
    unnamed x1, blocking collectives  13.7 us
    dot_general x1, matrix products, local(): lax.dot_general(column_block, gathered, (((0,), (0,)), ((), ())), preferr...  8.53 us
    dot_general x1, matrix products, local(): jnp.dot(inputs, table_in, preferred_element_type=jnp.float32)  5.35 us

commit v1 on v0

v1 whole, which is shorter than its diff:
```python
import functools
import math

import jax
import jax.numpy as jnp
from jax import lax
from jax.experimental import pallas as pl
from jax.experimental.pallas import tpu as pltpu
from jax.sharding import PartitionSpec as P

K_IN = 64
K_OUT = 128
PRIME = 65521
HALF = 32760
INV = pow(3571, -1, PRIME)
STEP_R = 7919 * INV % PRIME
STEP_S = 9973 * INV % PRIME
LANES = 128
HASH_ROWS = 640
CHUNK = 1024
damp_ratio = 0.5
MESH = pl.DeviceIdType.MESH


def fold(x):
    return (x & 65535) + (x >> 16) * 15


def wrap(x):
    return jnp.where(x >= PRIME, x - PRIME, x)


def hash_row(rows):
    g = lax.broadcasted_iota(jnp.int32, (rows, LANES), 0) * LANES + lax.broadcasted_iota(
        jnp.int32, (rows, LANES), 1
    )
    g = wrap(g)
    h1 = wrap(fold(g * 3571))
    m = h1 - ((h1 * 8241) >> 22) * 509
    m = jnp.where(m < 0, m + 509, m)
    h2 = fold(h1 * (m + 17))
    return wrap(fold(h2 * 97 + g)).astype(jnp.float32)


def make_table(hash_ref, table_ref, seed, count, fan_in):
    depth = fan_in // LANES
    scale = math.sqrt(3.0 / fan_in) / HALF
    lane = lax.broadcasted_iota(jnp.int32, (depth, LANES), 1)
    start = lax.rem(seed * STEP_S, PRIME)

    def body(r, offset):
        row = offset >> 7
        shift = offset & 127
        c = 31 * r - offset
        c = jnp.where(c < 0, c + PRIME, c)
        add = (c - HALF).astype(jnp.float32)
        x = jnp.where(
            lane >= shift, hash_ref[pl.ds(row, depth), :], hash_ref[pl.ds(row + 1, depth), :]
        )
        y = x + add
        y = jnp.where(y > HALF, y - PRIME, y) * scale
        table_ref[pl.ds(r, depth, stride=count), :] = pltpu.roll(y, (128 - shift) & 127, 1)
        offset = offset + STEP_R
        return jnp.where(offset >= PRIME, offset - PRIME, offset)

    lax.fori_loop(0, count, body, start, unroll=4)


def table_block(table_ref, count, first, blocks):
    return jnp.concatenate(
        [
            table_ref[(first + b) * count : (first + b + 1) * count, :].astype(jnp.bfloat16)
            for b in range(blocks)
        ],
        axis=1,
    )


def nt_dot(a, b):
    return lax.dot_general(a, b, (((1,), (1,)), ((), ())), preferred_element_type=jnp.float32)


def project_kernel(
    seeds, lengths, in_hbm, og_hbm, grad_ref, hash_ref, tin, tout, inbuf, ogbuf, in_sem, og_sem
):
    tokens, d_in = in_hbm.shape
    d_out = og_hbm.shape[1]
    chunks = d_out // CHUNK
    in_copy = pltpu.make_async_copy(in_hbm, inbuf, in_sem)
    in_copy.start()
    copies = []
    for c in range(chunks):
        cols = pl.ds(c * CHUNK, CHUNK)
        copy = pltpu.make_async_copy(og_hbm.at[:, cols], ogbuf.at[:, cols], og_sem.at[c])
        copy.start()
        copies.append(copy)
    hash_ref[...] = hash_row(HASH_ROWS)
    make_table(hash_ref, tin, seeds[0], K_IN, d_in)
    make_table(hash_ref, tout, seeds[1], K_OUT, d_out)
    in_copy.wait()
    per = CHUNK // LANES
    proj_in = jnp.zeros((K_IN, tokens), jnp.float32)
    for c in range(d_in // CHUNK):
        proj_in += nt_dot(
            table_block(tin, K_IN, c * per, per), inbuf[:, c * CHUNK : (c + 1) * CHUNK]
        )
    proj_out = jnp.zeros((K_OUT, tokens), jnp.float32)
    for c in range(chunks):
        copies[c].wait()
        proj_out += nt_dot(
            table_block(tout, K_OUT, c * per, per), ogbuf[:, c * CHUNK : (c + 1) * CHUNK]
        )
    live = lax.broadcasted_iota(jnp.int32, (K_IN, tokens), 1) < lengths[0]
    proj_in = jnp.where(live, proj_in, 0.0).astype(jnp.bfloat16)
    outer = nt_dot(proj_in, proj_out.astype(jnp.bfloat16))
    grad_ref[...] = (outer * (1.0 / math.sqrt(tokens))).astype(jnp.bfloat16)


def gather_kernel(n, ids, grad, gat, gid, send, recv, id_send, id_recv):
    me = lax.axis_index("param")
    chips = n // 2
    chip, core = me // 2, lax.rem(me, 2)
    sibling = chip * 2 + 1 - core
    peers = [lax.rem(chip + off, chips) * 2 + core for off in range(1, chips)]

    barrier = pltpu.get_barrier_semaphore()
    for peer in [sibling] + peers:
        pl.semaphore_signal(barrier, inc=1, device_id={"param": peer}, device_id_type=MESH)
    gat[me] = grad[...]
    gid[me] = jnp.zeros((1, LANES), jnp.int32) + ids[0]
    pl.semaphore_wait(barrier, chips)

    def push(block, target, slot):
        out = []
        for ref, s, r in ((gid, id_send, id_recv), (gat, send, recv)):
            copy = pltpu.make_async_remote_copy(
                src_ref=ref.at[block],
                dst_ref=ref.at[block],
                send_sem=s.at[slot],
                recv_sem=r.at[block],
                device_id={"param": target},
                device_id_type=MESH,
            )
            copy.start()
            out.append(copy)
        return out

    def arrived(block):
        for ref, s, r in ((gid, id_send, id_recv), (gat, send, recv)):
            pltpu.make_async_remote_copy(
                src_ref=ref.at[block],
                dst_ref=ref.at[block],
                send_sem=s.at[0],
                recv_sem=r.at[block],
                device_id={"param": sibling},
                device_id_type=MESH,
            ).wait_recv()

    started = []
    for off, peer in enumerate(peers):
        started += push(me, peer, off)
    started += push(me, sibling, chips - 1)
    for off in range(1, chips):
        block = lax.rem(chip - off + chips, chips) * 2 + core
        arrived(block)
        started += push(block, sibling, chips - 1 + off)
    for off in range(chips):
        arrived(lax.rem(chip - off + chips, chips) * 2 + 1 - core)
    for copy in started:
        copy.wait_send()


def finish_kernel(n, gat, gid, fisher, precond, kernel, wide, low, rows, prec, fbuf, sem):
    me = lax.axis_index("param")
    width = K_IN * K_OUT
    block = width // n
    wide[...] = gat[...].astype(jnp.float32).reshape(n * K_IN, K_OUT)
    for i in range(K_IN):
        low[:, i * K_OUT : (i + 1) * K_OUT] = wide[pl.ds(i, n, stride=K_IN), :].astype(jnp.bfloat16)
    first = me * block
    for i in range(max(1, block // K_OUT)):
        part = wide[pl.ds(first // K_OUT + i, n, stride=K_IN), :] * (1.0 / n)
        if block < K_OUT:
            part = pltpu.roll(part, lax.rem(K_OUT - lax.rem(first, K_OUT), K_OUT), 1)
        rows[i * K_OUT : (i + 1) * K_OUT, :] = part.T.astype(jnp.bfloat16)
    columns = rows[0:block, :]
    copies = []
    for c in range(width // CHUNK):
        cols = pl.ds(c * CHUNK, CHUNK)
        fbuf[:, cols] = jnp.dot(columns, low[:, cols], preferred_element_type=jnp.float32)
        copy = pltpu.make_async_copy(fbuf.at[:, cols], fisher.at[:, cols], sem.at[c])
        copy.start()
        copies.append(copy)

    gram = jnp.zeros((n, n), jnp.float32)
    for c in range(width // CHUNK):
        cols = pl.ds(c * CHUNK, CHUNK)
        gram += nt_dot(low[:, cols], low[:, cols])
    sub = lax.broadcasted_iota(jnp.int32, (n, n), 0)
    lane = lax.broadcasted_iota(jnp.int32, (n, n), 1)
    eye = sub == lane
    square_sum = jnp.sum(jnp.where(eye, gram, 0.0), keepdims=True)
    damping = damp_ratio * square_sum / (n * width)
    system = gram + jnp.where(eye, damping * n, 0.0)

    def sweep(k, m):
        col = jnp.sum(jnp.where(lane == k, m, 0.0), axis=1, keepdims=True)
        row = jnp.sum(jnp.where(sub == k, m, 0.0), axis=0, keepdims=True)
        pivot = 1.0 / jnp.sum(jnp.where(eye & (sub == k), m, 0.0), keepdims=True)
        scaled = row * pivot
        out = m - col * scaled
        out = jnp.where(sub == k, scaled, out)
        out = jnp.where(lane == k, col * pivot, out)
        return jnp.where(eye & (sub == k), -pivot, out)

    if n <= 16:
        for k in range(n):
            system = sweep(k, system)
    else:
        system = lax.fori_loop(0, n, sweep, system)
    inverse = system * (-float(n))
    high = inverse.astype(jnp.bfloat16)
    rest = inverse - high.astype(jnp.float32)
    mid = rest.astype(jnp.bfloat16)
    last = (rest - mid.astype(jnp.float32)).astype(jnp.bfloat16)
    pair = jnp.zeros((n, n), jnp.float32)
    for c in range(width // CHUNK):
        cols = pl.ds(c * CHUNK, CHUNK)
        g = low[:, cols]
        p = jnp.dot(last, g, preferred_element_type=jnp.float32)
        p += jnp.dot(mid, g, preferred_element_type=jnp.float32)
        p += jnp.dot(high, g, preferred_element_type=jnp.float32)
        prec[:, cols] = p
        pair += nt_dot(p.astype(jnp.bfloat16), g)
    precond[...] = prec[pl.ds(me, 1), :]
    ids = gid[:, 0, :][:, 0:n]
    own = jnp.sum(jnp.where(eye & (ids == me), 1.0, 0.0), axis=0, keepdims=True)
    by_slot = jnp.sum(pair * own, axis=1, keepdims=True)
    kernel[...] = jnp.sum(jnp.where(ids == lane, by_slot, 0.0), axis=0, keepdims=True) * (
        1.0 / width
    )
    for copy in copies:
        copy.wait()


def vmem(shape, dtype=jnp.float32):
    return pltpu.VMEM(shape, dtype)


def local(n, inputs, out_grads, lengths, example_ids, proj_seeds):
    any_space = pl.BlockSpec(memory_space=pl.ANY)
    smem = pl.BlockSpec(memory_space=pltpu.SMEM)
    vm = pl.BlockSpec(memory_space=pltpu.VMEM)
    tokens, d_in = inputs.shape
    d_out = out_grads.shape[1]
    width = K_IN * K_OUT
    grads = pl.pallas_call(
        project_kernel,
        out_shape=jax.ShapeDtypeStruct((K_IN, K_OUT), jnp.bfloat16),
        in_specs=[smem, smem, any_space, any_space],
        out_specs=vm,
        scratch_shapes=[
            vmem((HASH_ROWS, LANES)),
            vmem((d_in // LANES * K_IN, LANES)),
            vmem((d_out // LANES * K_OUT, LANES)),
            vmem((tokens, d_in), jnp.bfloat16),
            vmem((tokens, d_out), jnp.bfloat16),
            pltpu.SemaphoreType.DMA,
            pltpu.SemaphoreType.DMA((d_out // CHUNK,)),
        ],
        compiler_params=pltpu.CompilerParams(vmem_limit_bytes=56 << 20),
    )(proj_seeds, lengths, inputs, out_grads)
    gat, gid = pl.pallas_call(
        functools.partial(gather_kernel, n),
        out_shape=(
            jax.ShapeDtypeStruct((n, K_IN, K_OUT), jnp.bfloat16),
            jax.ShapeDtypeStruct((n, 1, LANES), jnp.int32),
        ),
        in_specs=[smem, vm],
        out_specs=(vm, vm),
        scratch_shapes=[
            pltpu.SemaphoreType.DMA((n,)),
            pltpu.SemaphoreType.DMA((n,)),
            pltpu.SemaphoreType.DMA((n,)),
            pltpu.SemaphoreType.DMA((n,)),
        ],
        compiler_params=pltpu.CompilerParams(collective_id=0, has_side_effects=True),
    )(example_ids, grads)
    return pl.pallas_call(
        functools.partial(finish_kernel, n),
        out_shape=(
            jax.ShapeDtypeStruct((width // n, width), jnp.float32),
            jax.ShapeDtypeStruct((1, width), jnp.float32),
            jax.ShapeDtypeStruct((1, n), jnp.float32),
        ),
        in_specs=[vm, vm],
        out_specs=(any_space, vm, vm),
        scratch_shapes=[
            vmem((n * K_IN, K_OUT)),
            vmem((n, width), jnp.bfloat16),
            vmem((max(width // n, K_OUT), n), jnp.bfloat16),
            vmem((n, width)),
            vmem((width // n, width)),
            pltpu.SemaphoreType.DMA((width // CHUNK,)),
        ],
        compiler_params=pltpu.CompilerParams(vmem_limit_bytes=48 << 20),
    )(gat, gid)


def solution(mesh):
    rows = P(("parts", "param"), None)
    flat = P(("parts", "param"))
    return jax.shard_map(
        functools.partial(local, mesh.shape["param"]),
        mesh=mesh,
        in_specs=(rows, rows, flat, flat, P("parts")),
        out_specs=(rows, rows, rows),
        check_vma=False,
    )
```

time: 118 us -> 42.9 us (0.36)
  blocking collectives: 52.1 us -> 0 us
  matrix products: 47.6 us -> 0 us
  Pallas kernels: 0 us -> 38.9 us
  other arithmetic: 6.11 us -> 0 us
  between operations: 6.76 us -> 1.95 us
  local copies, waits for them, and re-layouts: 5.43 us -> 1.64 us
    dot_general x7 -> x0, matrix products: 47.2 us -> none  [the longest x1 32.5 us: local(): jnp.dot(out_grads, table_out, preferred_element_type=jnp.float32)]
    pallas_call x0 -> x3, Pallas kernels: none -> 38.9 us  [the longest x1 19.6 us: local(): pl.pallas_call(project_kernel, out_shape=jax.ShapeDtypeStruct((K_IN, K_OU...]
    all_gather x2 -> x0, blocking collectives: 38.4 us -> none  [the longest x1 19.4 us: local(): lax.all_gather(gradients, 'param', axis=0, tiled=True)]
    unnamed x1 -> x0, blocking collectives: 13.7 us -> none
    another operation x5 -> x0, other arithmetic: 4.03 us -> none  [the longest x3 2.15 us: local(): factor = jnp.linalg.cholesky(system)]
    slice x1 -> x0, local copies, waits for them, and re-layouts: 1.31 us -> none  [local(): table_out = projection_table(K_OUT, out_grads.shape[1], proj_seeds[1])]
    scatter x2 -> x0, local copies, waits for them, and re-layouts: 1.26 us -> none  [the longest x1 0.64 us: local(): jnp.zeros((ex_dev, example_count), jnp.float32).at[:, all_ids]]
where the time goes in v1:
time: 42.9 us; the launch traced here: 42.5 us
  Pallas kernels  38.9 us (91%)
  between operations  1.95 us (5%)
  local copies, waits for them, and re-layouts  1.64 us (4%)
    pallas_call x1, Pallas kernels, local(): pl.pallas_call(project_kernel, out_shape=jax.ShapeDtypeStruct((K_IN, K_OU...  19.6 us
    pallas_call x1, Pallas kernels, local(): pl.pallas_call(functools.partial(gather_kernel, n), out_shape=(jax.ShapeD...  12.2 us
    pallas_call x1, Pallas kernels, local(): pl.pallas_call(functools.partial(finish_kernel, n), out_shape=(jax.ShapeD...  7.1 us
    unnamed x4, local copies, waits for them, and re-layouts  1.64 us

profile of v1, /device:TPU:0, one launch (start us, length us, event | category | flops | bytes accessed | tf_op | source)
XLA Modules:
  0.0 42.5 jit_solution(17927128065647083700)
XLA Ops:
  1.9 19.6 %shard_map.76.grad = bf16[64,128]{1,0:T(8,128)(2,1)} custom-call(s32[2]{0:T(128)} %seeds.1, s32[1]{0:T(128)S(6)} %copy.8.lengths, bf16[256,4096]{1,0:T(8,128)(2,1)} %in_hbm.1, bf16[256,14336]{1,0:T(8,128)(2,1)} %og_hbm.1), custom_call_target="tpu_custom_call" | custom-call | tf_op jit(solution)/shard_map/pallas_call | solution.py:257
  21.5 12.2 %shard_map.77 = (bf16[16,64,128]{2,1,0:T(8,128)(2,1)}, s32[16,1,128]{2,1,0:T(1,128)}) custom-call(s32[1]{0:T(128)S(6)} %copy.9.ids, bf16[64,128]{1,0:T(8,128)(2,1)} %shard_map.76.grad), custom_call_target="tpu_custom_call" | custom-call | tf_op jit(solution)/shard_map/pallas_call | solution.py:273
  33.8 0.0 copy-start
  33.8 0.9 %copy-done = bf16[16,64,128]{2,1,0:T(8,128)(2,1)S(1)} copy-done((bf16[16,64,128]{2,1,0:T(8,128)(2,1)S(1)}, bf16[16,64,128]{2,1,0:T(8,128)(2,1)}, u32[]{:S(2)}) %copy-start) | copy-done | bytes 262168
  34.7 0.0 copy-start.1
  34.7 0.7 %copy-done.1 = s32[16,1,128]{2,1,0:T(1,128)S(1)} copy-done((s32[16,1,128]{2,1,0:T(1,128)S(1)}, s32[16,1,128]{2,1,0:T(1,128)}, u32[]{:S(2)}) %copy-start.1) | copy-done | bytes 8216
  35.4 7.1 %shard_map.78 = (f32[512,8192]{1,0:T(8,128)}, f32[1,8192]{1,0:T(1,128)}, f32[1,16]{1,0:T(1,128)}) custom-call(bf16[16,64,128]{2,1,0:T(8,128)(2,1)S(1)} %copy-done, s32[16,1,128]{2,1,0:T(1,128)S(1)} %copy-done.1), custom_call_target="tpu_custom_call" | custom-call | tf_op jit(solution)/shard_map/pallas_call | solution.py:289
Async XLA Ops:
  33.8 1.0 %copy-start = (bf16[16,64,128]{2,1,0:T(8,128)(2,1)S(1)}, bf16[16,64,128]{2,1,0:T(8,128)(2,1)}, u32[]{:S(2)}) copy-start(bf16[16,64,128]{2,1,0:T(8,128)(2,1)} %get-tuple-element.5.gat) | copy-start | bytes 786436
  34.7 0.7 %copy-start.1 = (s32[16,1,128]{2,1,0:T(1,128)S(1)}, s32[16,1,128]{2,1,0:T(1,128)}, u32[]{:S(2)}) copy-start(s32[16,1,128]{2,1,0:T(1,128)} %get-tuple-element.6.gid) | copy-start | bytes 24580

commit v2 on v1

v2 whole, which is shorter than its diff:
```python
import functools
import math

import jax
import jax.numpy as jnp
from jax import lax
from jax.experimental import pallas as pl
from jax.experimental.pallas import tpu as pltpu
from jax.sharding import PartitionSpec as P

K_IN = 64
K_OUT = 128
PRIME = 65521
HALF = 32760
INV = pow(3571, -1, PRIME)
STEP_R = 7919 * INV % PRIME
STEP_S = 9973 * INV % PRIME
LANES = 128
HASH_ROWS = 640
CHUNK = 1024
PAD = 8
damp_ratio = 0.5
MESH = pl.DeviceIdType.MESH


def fold(x):
    return (x & 65535) + (x >> 16) * 15


def wrap(x):
    return jnp.where(x >= PRIME, x - PRIME, x)


def hash_row(rows):
    g = lax.broadcasted_iota(jnp.int32, (rows, LANES), 0) * LANES + lax.broadcasted_iota(
        jnp.int32, (rows, LANES), 1
    )
    g = wrap(g)
    h1 = wrap(fold(g * 3571))
    m = h1 - ((h1 * 8241) >> 22) * 509
    m = jnp.where(m < 0, m + 509, m)
    h2 = fold(h1 * (m + 17))
    return wrap(fold(h2 * 97 + g)).astype(jnp.float32)


def make_table(hash_ref, table_ref, seed, count, fan_in):
    depth = fan_in // LANES
    scale = math.sqrt(3.0 / fan_in) / HALF
    lane = lax.broadcasted_iota(jnp.int32, (depth, LANES), 1)
    start = lax.rem(seed * STEP_S, PRIME)

    def body(r, offset):
        row = offset >> 7
        shift = offset & 127
        c = 31 * r - offset
        c = jnp.where(c < 0, c + PRIME, c)
        add = (c - HALF).astype(jnp.float32)
        x = jnp.where(
            lane >= shift, hash_ref[pl.ds(row, depth), :], hash_ref[pl.ds(row + 1, depth), :]
        )
        y = x + add
        y = jnp.where(y > HALF, y - PRIME, y) * scale
        table_ref[pl.ds(r, depth, stride=count + PAD), :] = pltpu.roll(y, (128 - shift) & 127, 1)
        offset = offset + STEP_R
        return jnp.where(offset >= PRIME, offset - PRIME, offset)

    lax.fori_loop(0, count, body, start, unroll=8)


def table_block(table_ref, count, first, blocks):
    return jnp.concatenate(
        [
            table_ref[(first + b) * (count + PAD) : (first + b) * (count + PAD) + count, :].astype(
                jnp.bfloat16
            )
            for b in range(blocks)
        ],
        axis=1,
    )


def nt_dot(a, b):
    return lax.dot_general(a, b, (((1,), (1,)), ((), ())), preferred_element_type=jnp.float32)


def project_gather_kernel(
    n,
    seeds,
    lengths,
    ids,
    in_hbm,
    og_hbm,
    gat,
    gid,
    hash_ref,
    tin,
    tout,
    inbuf,
    ogbuf,
    in_sem,
    og_sem,
    send,
    recv,
    id_send,
    id_recv,
):
    me = lax.axis_index("param")
    chips = n // 2
    chip, core = me // 2, lax.rem(me, 2)
    sibling = chip * 2 + 1 - core
    peers = [lax.rem(chip + off, chips) * 2 + core for off in range(1, chips)]
    grad_lane, id_lane = (gat, send, recv), (gid, id_send, id_recv)

    barrier = pltpu.get_barrier_semaphore()
    for peer in [sibling] + peers:
        pl.semaphore_signal(barrier, inc=1, device_id={"param": peer}, device_id_type=MESH)

    def push(lane, block, target, slot):
        ref, s, r = lane
        copy = pltpu.make_async_remote_copy(
            src_ref=ref.at[block],
            dst_ref=ref.at[block],
            send_sem=s.at[slot],
            recv_sem=r.at[block],
            device_id={"param": target},
            device_id_type=MESH,
        )
        copy.start()
        return copy

    def arrived(lane, block):
        ref, s, r = lane
        pltpu.make_async_remote_copy(
            src_ref=ref.at[block],
            dst_ref=ref.at[block],
            send_sem=s.at[0],
            recv_sem=r.at[block],
            device_id={"param": sibling},
            device_id_type=MESH,
        ).wait_recv()

    def send_own(lane):
        out = [push(lane, me, peer, off) for off, peer in enumerate(peers)]
        return out + [push(lane, me, sibling, chips - 1)]

    def forward(lane):
        out = []
        for off in range(1, chips):
            block = lax.rem(chip - off + chips, chips) * 2 + core
            arrived(lane, block)
            out.append(push(lane, block, sibling, chips - 1 + off))
        return out

    def collect(lane):
        for off in range(chips):
            arrived(lane, lax.rem(chip - off + chips, chips) * 2 + 1 - core)

    tokens, d_in = in_hbm.shape
    d_out = og_hbm.shape[1]
    in_copy = pltpu.make_async_copy(in_hbm, inbuf, in_sem)
    in_copy.start()
    og_copy = pltpu.make_async_copy(og_hbm, ogbuf, og_sem)
    og_copy.start()
    gid[me] = jnp.zeros((1, LANES), jnp.int32) + ids[0]
    hash_ref[...] = hash_row(HASH_ROWS)
    make_table(hash_ref, tin, seeds[0], K_IN, d_in)
    pl.semaphore_wait(barrier, chips)
    started = send_own(id_lane)
    make_table(hash_ref, tout, seeds[1], K_OUT, d_out)
    started += forward(id_lane)
    per = CHUNK // LANES
    in_copy.wait()
    proj_in = jnp.zeros((tokens, K_IN), jnp.float32)
    for c in range(d_in // CHUNK):
        proj_in += nt_dot(
            inbuf[:, c * CHUNK : (c + 1) * CHUNK], table_block(tin, K_IN, c * per, per)
        )
    og_copy.wait()
    proj_out = jnp.zeros((tokens, K_OUT), jnp.float32)
    for c in range(d_out // CHUNK):
        proj_out += nt_dot(
            ogbuf[:, c * CHUNK : (c + 1) * CHUNK], table_block(tout, K_OUT, c * per, per)
        )
    live = lax.broadcasted_iota(jnp.int32, (tokens, K_IN), 0) < lengths[0]
    proj_in = jnp.where(live, proj_in, 0.0).T.astype(jnp.bfloat16)
    outer = jnp.dot(proj_in, proj_out.astype(jnp.bfloat16), preferred_element_type=jnp.float32)
    gat[me] = (outer * (1.0 / math.sqrt(tokens))).astype(jnp.bfloat16)
    started += send_own(grad_lane)
    collect(id_lane)
    started += forward(grad_lane)
    collect(grad_lane)
    for copy in started:
        copy.wait_send()


def finish_kernel(
    n, gat_any, gid_any, fisher, precond, kernel, gat, gid, wide, low, rows, prec, fbuf, sem, arg_sem
):
    gat_copy = pltpu.make_async_copy(gat_any, gat, arg_sem.at[0])
    gat_copy.start()
    gid_copy = pltpu.make_async_copy(gid_any, gid, arg_sem.at[1])
    gid_copy.start()
    me = lax.axis_index("param")
    width = K_IN * K_OUT
    block = width // n
    gat_copy.wait()
    wide[...] = gat[...].astype(jnp.float32).reshape(n * K_IN, K_OUT)
    for i in range(K_IN):
        low[:, i * K_OUT : (i + 1) * K_OUT] = wide[pl.ds(i, n, stride=K_IN), :].astype(jnp.bfloat16)
    first = me * block
    for i in range(max(1, block // K_OUT)):
        part = wide[pl.ds(first // K_OUT + i, n, stride=K_IN), :] * (1.0 / n)
        if block < K_OUT:
            part = pltpu.roll(part, lax.rem(K_OUT - lax.rem(first, K_OUT), K_OUT), 1)
        rows[i * K_OUT : (i + 1) * K_OUT, :] = part.T.astype(jnp.bfloat16)
    columns = rows[0:block, :]
    copies = []
    for c in range(width // CHUNK):
        cols = pl.ds(c * CHUNK, CHUNK)
        fbuf[:, cols] = jnp.dot(columns, low[:, cols], preferred_element_type=jnp.float32)
        copy = pltpu.make_async_copy(fbuf.at[:, cols], fisher.at[:, cols], sem.at[c])
        copy.start()
        copies.append(copy)

    gram = jnp.zeros((n, n), jnp.float32)
    for c in range(width // CHUNK):
        cols = pl.ds(c * CHUNK, CHUNK)
        gram += nt_dot(low[:, cols], low[:, cols])
    sub = lax.broadcasted_iota(jnp.int32, (n, n), 0)
    lane = lax.broadcasted_iota(jnp.int32, (n, n), 1)
    eye = sub == lane
    square_sum = jnp.sum(jnp.where(eye, gram, 0.0), keepdims=True)
    damping = damp_ratio * square_sum / (n * width)
    system = gram + jnp.where(eye, damping * n, 0.0)

    def sweep(k, m):
        col = jnp.sum(jnp.where(lane == k, m, 0.0), axis=1, keepdims=True)
        row = jnp.sum(jnp.where(sub == k, m, 0.0), axis=0, keepdims=True)
        pivot = 1.0 / jnp.sum(jnp.where(eye & (sub == k), m, 0.0), keepdims=True)
        scaled = row * pivot
        out = m - col * scaled
        out = jnp.where(sub == k, scaled, out)
        out = jnp.where(lane == k, col * pivot, out)
        return jnp.where(eye & (sub == k), -pivot, out)

    if n <= 16:
        for k in range(n):
            system = sweep(k, system)
    else:
        system = lax.fori_loop(0, n, sweep, system)
    inverse = system * (-float(n))
    high = inverse.astype(jnp.bfloat16)
    rest = inverse - high.astype(jnp.float32)
    mid = rest.astype(jnp.bfloat16)
    last = (rest - mid.astype(jnp.float32)).astype(jnp.bfloat16)
    pair = jnp.zeros((n, n), jnp.float32)
    for c in range(width // CHUNK):
        cols = pl.ds(c * CHUNK, CHUNK)
        g = low[:, cols]
        p = jnp.dot(last, g, preferred_element_type=jnp.float32)
        p += jnp.dot(mid, g, preferred_element_type=jnp.float32)
        p += jnp.dot(high, g, preferred_element_type=jnp.float32)
        prec[:, cols] = p
        pair += nt_dot(p.astype(jnp.bfloat16), g)
    precond[...] = prec[pl.ds(me, 1), :]
    gid_copy.wait()
    ids = gid[:, 0, :][:, 0:n]
    own = jnp.sum(jnp.where(eye & (ids == me), 1.0, 0.0), axis=0, keepdims=True)
    by_slot = jnp.sum(pair * own, axis=1, keepdims=True)
    kernel[...] = jnp.sum(jnp.where(ids == lane, by_slot, 0.0), axis=0, keepdims=True) * (
        1.0 / width
    )
    for copy in copies:
        copy.wait()


def vmem(shape, dtype=jnp.float32):
    return pltpu.VMEM(shape, dtype)


def local(n, inputs, out_grads, lengths, example_ids, proj_seeds):
    any_space = pl.BlockSpec(memory_space=pl.ANY)
    smem = pl.BlockSpec(memory_space=pltpu.SMEM)
    vm = pl.BlockSpec(memory_space=pltpu.VMEM)
    tokens, d_in = inputs.shape
    d_out = out_grads.shape[1]
    width = K_IN * K_OUT
    gat, gid = pl.pallas_call(
        functools.partial(project_gather_kernel, n),
        out_shape=(
            jax.ShapeDtypeStruct((n, K_IN, K_OUT), jnp.bfloat16),
            jax.ShapeDtypeStruct((n, 1, LANES), jnp.int32),
        ),
        in_specs=[smem, smem, smem, any_space, any_space],
        out_specs=(vm, vm),
        scratch_shapes=[
            vmem((HASH_ROWS, LANES)),
            vmem((d_in // LANES * (K_IN + PAD), LANES)),
            vmem((d_out // LANES * (K_OUT + PAD), LANES)),
            vmem((tokens, d_in), jnp.bfloat16),
            vmem((tokens, d_out), jnp.bfloat16),
            pltpu.SemaphoreType.DMA,
            pltpu.SemaphoreType.DMA,
            pltpu.SemaphoreType.DMA((n,)),
            pltpu.SemaphoreType.DMA((n,)),
            pltpu.SemaphoreType.DMA((n,)),
            pltpu.SemaphoreType.DMA((n,)),
        ],
        compiler_params=pltpu.CompilerParams(
            collective_id=0, has_side_effects=True, vmem_limit_bytes=60 << 20
        ),
    )(proj_seeds, lengths, example_ids, inputs, out_grads)
    return pl.pallas_call(
        functools.partial(finish_kernel, n),
        out_shape=(
            jax.ShapeDtypeStruct((width // n, width), jnp.float32),
            jax.ShapeDtypeStruct((1, width), jnp.float32),
            jax.ShapeDtypeStruct((1, n), jnp.float32),
        ),
        in_specs=[any_space, any_space],
        out_specs=(any_space, vm, vm),
        scratch_shapes=[
            vmem((n, K_IN, K_OUT), jnp.bfloat16),
            vmem((n, 1, LANES), jnp.int32),
            vmem((n * K_IN, K_OUT)),
            vmem((n, width), jnp.bfloat16),
            vmem((max(width // n, K_OUT), n), jnp.bfloat16),
            vmem((n, width)),
            vmem((width // n, width)),
            pltpu.SemaphoreType.DMA((width // CHUNK,)),
            pltpu.SemaphoreType.DMA((2,)),
        ],
        compiler_params=pltpu.CompilerParams(vmem_limit_bytes=60 << 20),
    )(gat, gid)


def solution(mesh):
    rows = P(("parts", "param"), None)
    flat = P(("parts", "param"))
    return jax.shard_map(
        functools.partial(local, mesh.shape["param"]),
        mesh=mesh,
        in_specs=(rows, rows, flat, flat, P("parts")),
        out_specs=(rows, rows, rows),
        check_vma=False,
    )
```

time: 42.9 us -> 31.1 us (0.72)
  Pallas kernels: 38.9 us -> 29 us
  local copies, waits for them, and re-layouts: 1.64 us -> 0 us
    pallas_call x2 -> x1, Pallas kernels: 31.8 us -> 20.9 us  [local(): pl.pallas_call(functools.partial(project_gather_kernel, n), out_shape=(ja...]
    unnamed x4 -> x0, local copies, waits for them, and re-layouts: 1.64 us -> none
    pallas_call x1, Pallas kernels: 7.1 us -> 8.07 us  [local(): pl.pallas_call(functools.partial(finish_kernel, n), out_shape=(jax.ShapeD...]
where the time goes in v2:
time: 31.1 us; the launch traced here: 30.9 us
  Pallas kernels  29 us (93%)
  between operations  1.93 us (6%)
    pallas_call x1, Pallas kernels, local(): pl.pallas_call(functools.partial(project_gather_kernel, n), out_shape=(ja...  20.9 us
    pallas_call x1, Pallas kernels, local(): pl.pallas_call(functools.partial(finish_kernel, n), out_shape=(jax.ShapeD...  8.07 us

profile of v2, /device:TPU:0, one launch (start us, length us, event | category | flops | bytes accessed | tf_op | source)
XLA Modules:
  0.0 30.9 jit_solution(1572069489653138086)
XLA Ops:
  1.9 20.9 %shard_map.76 = (bf16[16,64,128]{2,1,0:T(8,128)(2,1)}, s32[16,1,128]{2,1,0:T(1,128)}) custom-call(s32[2]{0:T(128)} %seeds.1, s32[1]{0:T(128)S(6)} %copy.8.lengths, s32[1]{0:T(128)S(6)} %copy.9.ids, bf16[256,4096]{1,0:T(8,128)(2,1)} %in_hbm.1, bf16[256,14336]{1,0:T(8,128)(2,1)} %og_hbm.1), custom_call_target="tpu_custom_call" | custom-call | tf_op jit(solution)/shard_map/pallas_call | solution.py:288
  22.8 8.1 %shard_map.77 = (f32[512,8192]{1,0:T(8,128)}, f32[1,8192]{1,0:T(1,128)}, f32[1,16]{1,0:T(1,128)}) custom-call(bf16[16,64,128]{2,1,0:T(8,128)(2,1)} %get-tuple-element.5.gat_any, s32[16,1,128]{2,1,0:T(1,128)} %get-tuple-element.6.gid_any), custom_call_target="tpu_custom_call" | custom-call | tf_op jit(solution)/shard_map/pallas_call | solution.py:313

commit v3 on v2

--- a/solution.py
+++ b/solution.py
@@ -105,14 +105,11 @@
     id_recv,
 ):
     me = lax.axis_index("param")
-    chips = n // 2
-    chip, core = me // 2, lax.rem(me, 2)
-    sibling = chip * 2 + 1 - core
-    peers = [lax.rem(chip + off, chips) * 2 + core for off in range(1, chips)]
+    peers = [lax.rem(me + off, n) for off in range(1, n)]
     grad_lane, id_lane = (gat, send, recv), (gid, id_send, id_recv)
 
     barrier = pltpu.get_barrier_semaphore()
-    for peer in [sibling] + peers:
+    for peer in peers:
         pl.semaphore_signal(barrier, inc=1, device_id={"param": peer}, device_id_type=MESH)
 
     def push(lane, block, target, slot):
@@ -135,25 +132,16 @@
             dst_ref=ref.at[block],
             send_sem=s.at[0],
             recv_sem=r.at[block],
-            device_id={"param": sibling},
+            device_id={"param": lax.rem(me + 1, n)},
             device_id_type=MESH,
         ).wait_recv()
 
     def send_own(lane):
-        out = [push(lane, me, peer, off) for off, peer in enumerate(peers)]
-        return out + [push(lane, me, sibling, chips - 1)]
-
-    def forward(lane):
-        out = []
-        for off in range(1, chips):
-            block = lax.rem(chip - off + chips, chips) * 2 + core
-            arrived(lane, block)
-            out.append(push(lane, block, sibling, chips - 1 + off))
-        return out
+        return [push(lane, me, peer, off) for off, peer in enumerate(peers)]
 
     def collect(lane):
-        for off in range(chips):
-            arrived(lane, lax.rem(chip - off + chips, chips) * 2 + 1 - core)
+        for off in range(1, n):
+            arrived(lane, lax.rem(me + off, n))
 
     tokens, d_in = in_hbm.shape
     d_out = og_hbm.shape[1]
@@ -164,10 +152,9 @@
     gid[me] = jnp.zeros((1, LANES), jnp.int32) + ids[0]
     hash_ref[...] = hash_row(HASH_ROWS)
     make_table(hash_ref, tin, seeds[0], K_IN, d_in)
-    pl.semaphore_wait(barrier, chips)
+    pl.semaphore_wait(barrier, n - 1)
     started = send_own(id_lane)
     make_table(hash_ref, tout, seeds[1], K_OUT, d_out)
-    started += forward(id_lane)
     per = CHUNK // LANES
     in_copy.wait()
     proj_in = jnp.zeros((tokens, K_IN), jnp.float32)
@@ -187,7 +174,6 @@
     gat[me] = (outer * (1.0 / math.sqrt(tokens))).astype(jnp.bfloat16)
     started += send_own(grad_lane)
     collect(id_lane)
-    started += forward(grad_lane)
     collect(grad_lane)
     for copy in started:
         copy.wait_send()
@@ -204,7 +190,7 @@
     width = K_IN * K_OUT
     block = width // n
     gat_copy.wait()
-    wide[...] = gat[...].astype(jnp.float32).reshape(n * K_IN, K_OUT)
+    wide[0 : n * K_IN, :] = gat[...].astype(jnp.float32).reshape(n * K_IN, K_OUT)
     for i in range(K_IN):
         low[:, i * K_OUT : (i + 1) * K_OUT] = wide[pl.ds(i, n, stride=K_IN), :].astype(jnp.bfloat16)
     first = me * block
@@ -295,8 +281,8 @@
         out_specs=(vm, vm),
         scratch_shapes=[
             vmem((HASH_ROWS, LANES)),
-            vmem((d_in // LANES * (K_IN + PAD), LANES)),
-            vmem((d_out // LANES * (K_OUT + PAD), LANES)),
+            vmem(((d_in // LANES + 1) * (K_IN + PAD), LANES)),
+            vmem(((d_out // LANES + 1) * (K_OUT + PAD), LANES)),
             vmem((tokens, d_in), jnp.bfloat16),
             vmem((tokens, d_out), jnp.bfloat16),
             pltpu.SemaphoreType.DMA,
@@ -322,7 +308,7 @@
         scratch_shapes=[
             vmem((n, K_IN, K_OUT), jnp.bfloat16),
             vmem((n, 1, LANES), jnp.int32),
-            vmem((n * K_IN, K_OUT)),
+            vmem(((n + 1) * K_IN, K_OUT)),
             vmem((n, width), jnp.bfloat16),
             vmem((max(width // n, K_OUT), n), jnp.bfloat16),
             vmem((n, width)),

time: 31.1 us -> 30.4 us (0.977)
  Pallas kernels: 29 us -> 28.3 us
    pallas_call x1, Pallas kernels: 20.9 us -> 20.2 us  [local(): pl.pallas_call(functools.partial(project_gather_kernel, n), out_shape=(ja...]
where the time goes in v3:
time: 30.4 us; the launch traced here: 30.2 us
  Pallas kernels  28.3 us (93%)
  between operations  1.93 us (6%)
    pallas_call x1, Pallas kernels, local(): pl.pallas_call(functools.partial(project_gather_kernel, n), out_shape=(ja...  20.2 us
    pallas_call x1, Pallas kernels, local(): pl.pallas_call(functools.partial(finish_kernel, n), out_shape=(jax.ShapeD...  8.07 us

profile of v3, /device:TPU:0, one launch (start us, length us, event | category | flops | bytes accessed | tf_op | source)
XLA Modules:
  0.0 30.2 jit_solution(11779508105693039724)
XLA Ops:
  1.9 20.2 %shard_map.76 = (bf16[16,64,128]{2,1,0:T(8,128)(2,1)}, s32[16,1,128]{2,1,0:T(1,128)}) custom-call(s32[2]{0:T(128)} %seeds.1, s32[1]{0:T(128)S(6)} %copy.8.lengths, s32[1]{0:T(128)S(6)} %copy.9.ids, bf16[256,4096]{1,0:T(8,128)(2,1)} %in_hbm.1, bf16[256,14336]{1,0:T(8,128)(2,1)} %og_hbm.1), custom_call_target="tpu_custom_call" | custom-call | tf_op jit(solution)/shard_map/pallas_call | solution.py:274
  22.1 8.1 %shard_map.77 = (f32[512,8192]{1,0:T(8,128)}, f32[1,8192]{1,0:T(1,128)}, f32[1,16]{1,0:T(1,128)}) custom-call(bf16[16,64,128]{2,1,0:T(8,128)(2,1)} %get-tuple-element.5.gat_any, s32[16,1,128]{2,1,0:T(1,128)} %get-tuple-element.6.gid_any), custom_call_target="tpu_custom_call" | custom-call | tf_op jit(solution)/shard_map/pallas_call | solution.py:299
